TPU v7x, 32 devices: a whole 2x2x4 slice. The times are simulated.
32 devices in a mesh: mesh: 8 (over y, x, core), event: 4 (over z).
Axes of the slice: x: 2, y: 2, z: 4, core: 2. Of those that a mesh axis runs over, the one named last changes fastest.
Arguments:
- forward_now: float32 [4, 3, 20808], P('event', None, 'mesh'), may hold values from -6 to 6
- forward_prev: float32 [4, 3, 20808], P('event', None, 'mesh'), may hold values from -6 to 6
- adjoint_now: float32 [4, 3, 20808], P('event', None, 'mesh'), may hold values from -6 to 6
- adjoint_prev: float32 [4, 3, 20808], P('event', None, 'mesh'), may hold values from -6 to 6
- connectivity: int32 [125, 256], P(None, 'mesh'), may hold values from 0 to 2600, as said below
- lower_face: int32 [8, 289], P('mesh'), may hold values from 0 to 2600, as said below
- upper_face: int32 [8, 289], P('mesh'), may hold values from 0 to 2600, as said below
- bulk_modulus: float32 [125, 256], P(None, 'mesh'), may hold values from 0.5 to 2
- shear_modulus: float32 [125, 256], P(None, 'mesh'), may hold values from 0.3 to 1.2
- step_scale: float32 [20808], P('mesh'), may hold values from 0.0069 to 5.01, as said below
- receiver_points: int32 [1024], P('mesh'), may hold values from 0 to 2600
- adjoint_source: float32 [4, 2, 3, 1024], P('event', None, None, 'mesh'), may hold values from -18 to 18
Outputs:
- forward_next: float32 [4, 3, 20808], P('event', None, 'mesh')
- adjoint_next: float32 [4, 3, 20808], P('event', None, 'mesh')
- kernels: float32 [2, 125, 256], P(None, None, ('mesh', 'event'))
Inputs may be any that keep to these rules, and one draw needn't show every extreme that they name: `connectivity`: each column lists local point numbers of its element's partition; every local point is used. A partition's elements come in 2 layers of 16: the first layer holds every point of the partition's lower_face, the last layer every point of its upper_face, and no other element touches those points. `lower_face`: distinct local point numbers, none in upper_face of the same partition; slot s of partition p's lower_face and slot s of partition p-1's upper_face are one shared point. `upper_face`: distinct local point numbers, none in lower_face of the same partition. `step_scale`: Positive.
All inputs are finite; a program needn't handle non-finite values.
Results may differ from a plain program's by a relative error of at most 0.0001.
Values sent between devices are 32-bit elements; how exact they have to be, the bound alone decides.
A program may use at most 64 MiB of HBM per device.

v0:
```python
import functools
import math

import jax
import jax.numpy as jnp
import numpy as np
from jax import lax
from jax.experimental import pallas as pl
from jax.experimental.pallas import tpu as pltpu
from jax.sharding import PartitionSpec as P

STEPS = 2
LANES = 128
WIDE = 256
KERNEL_WEIGHT = 0.02
MESH = pl.DeviceIdType.MESH
TOP = lax.Precision.HIGHEST


def derivative_table():
    root = math.sqrt(3.0 / 7.0)
    points = [-1.0, -root, 0.0, root, 1.0]
    legendre = [(35.0 * x**4 - 30.0 * x**2 + 3.0) / 8.0 for x in points]
    table = np.zeros((5, 5))
    for row in range(5):
        for column in range(5):
            if row != column:
                table[row, column] = (
                    legendre[row] / legendre[column] / (points[row] - points[column])
                )
    table[0, 0] = -2.5
    table[4, 4] = 2.5
    return table


def cube_tables():
    deriv = derivative_table()
    line = np.array([0.1, 49.0 / 90.0, 32.0 / 45.0, 49.0 / 90.0, 0.1])
    cube = (line[:, None, None] * line[None, :, None] * line[None, None, :]).reshape(125)
    along = [
        np.kron(np.eye(25), deriv),
        np.kron(np.eye(5), np.kron(deriv, np.eye(5))),
        np.kron(deriv, np.eye(25)),
    ]
    ahead = np.zeros((LANES, 3 * LANES))
    back = np.zeros((3 * LANES, LANES))
    for i in range(3):
        ahead[:125, i * LANES : i * LANES + 125] = along[i].T
        back[i * LANES : i * LANES + 125, :125] = -along[i] * cube[:, None]
    return ahead.astype(np.float32), back.astype(np.float32)


def body(
    n_mesh,
    n_event,
    points,
    face,
    elems,
    fwd_now,
    fwd_prev,
    adj_now,
    adj_prev,
    conn,
    lower,
    upper,
    bulk_mod,
    shear_mod,
    scale,
    receivers,
    source,
    ahead,
    back,
    fwd_out,
    adj_out,
    kern_out,
    waves,
    before,
    scale_all,
    forces,
    packed,
    turned,
    rows,
    columns,
    onehot,
    left,
    stress_buf,
    force_buf,
    face_send,
    face_recv,
    kern_send,
    kern_recv,
    face_ssem,
    face_rsem,
    kern_ssem,
    kern_rsem,
):
    me = lax.axis_index("mesh")
    my_event = lax.axis_index("event")
    following = lax.rem(me + 1, n_mesh)
    previous = lax.rem(me + n_mesh - 1, n_mesh)
    barrier = pltpu.get_barrier_semaphore()
    for other in (following, previous):
        pl.semaphore_signal(
            barrier, inc=1, device_id={"mesh": other, "event": my_event}, device_id_type=MESH
        )
    for hop in range(1, n_event):
        peer = lax.rem(my_event + hop, n_event)
        pl.semaphore_signal(
            barrier, inc=1, device_id={"mesh": me, "event": peer}, device_id_type=MESH
        )

    f32 = jnp.float32
    chunks = -(-points // LANES)
    slabs = waves.shape[1] // WIDE
    face_chunks = face_send.shape[3] // LANES
    part_rows = left.shape[0] // 3
    cols = elems // n_event

    waves[...] = jnp.zeros_like(waves)
    before[...] = jnp.zeros_like(before)
    scale_all[...] = jnp.zeros_like(scale_all)
    waves[0:3, 0:points] = fwd_now[0]
    waves[3:6, 0:points] = adj_now[0]
    before[0:3, 0:points] = fwd_prev[0]
    before[3:6, 0:points] = adj_prev[0]
    scale_all[:, 0:points] = jnp.broadcast_to(scale[...], (8, points))

    packed[...] = jnp.zeros_like(packed)
    packed[0:125, 0:elems] = conn[...].astype(f32)
    packed[0:125, elems : 2 * elems] = bulk_mod[...]
    packed[0:125, 2 * elems : 3 * elems] = shear_mod[...]
    turned[...] = packed[...].T
    kappa = turned[elems : 2 * elems]
    mu = turned[2 * elems : 3 * elems]

    rows[...] = jnp.full(rows.shape, -1, jnp.int32)
    rows[0:1, :] = receivers[...]
    for which, ref in enumerate((lower, upper)):
        for k in range(face_chunks):
            size = min(LANES, face - k * LANES)
            at = 1 + which * face_chunks + k
            rows[at : at + 1, 0:size] = ref[:, k * LANES : k * LANES + size]
    columns[...] = rows[...].astype(f32).T.astype(jnp.int32)

    lane = lax.broadcasted_iota(jnp.int32, (LANES, WIDE), 1)

    def spread(at, column):
        low = column & (WIDE - 1)
        onehot[at * LANES : (at + 1) * LANES, :] = jnp.where(lane == low, 1.0, 0.0).astype(
            jnp.bfloat16
        )

    for e in range(elems):
        spread(e, packed[:, e : e + 1].astype(jnp.int32))
    for k in range(1 + 2 * face_chunks):
        spread(elems + k, columns[:, k : k + 1])

    def lookup(table, index, low, high):
        out = jnp.zeros(index.shape, f32)
        for k in range(chunks):
            got = jnp.take_along_axis(table(k), low, axis=1, mode="promise_in_bounds")
            out = jnp.where(high == k, got, out)
        return out

    def place(at, value, index):
        high = index >> 8
        first = value.astype(jnp.bfloat16).astype(f32)
        rest = value - first
        second = rest.astype(jnp.bfloat16).astype(f32)
        third = rest - second
        for s, part in enumerate((first, second, third)):
            slab = [jnp.where(high == k, part, 0.0) for k in range(part_rows // 8)]
            left[s * part_rows : (s + 1) * part_rows, at * LANES : (at + 1) * LANES] = (
                jnp.concatenate(slab, 0).astype(jnp.bfloat16)
            )

    def deposit(start, stop):
        span = slice(start * LANES, stop * LANES)
        total = jnp.dot(left[:, span], onehot[span, :], preferred_element_type=f32)
        return total[0:part_rows] + total[part_rows : 2 * part_rows] + total[2 * part_rows :]

    force_buf[...] = jnp.zeros_like(force_buf)
    bulk = jnp.zeros((elems, LANES), f32)
    shear = jnp.zeros((elems, LANES), f32)
    pending = []
    for step in range(STEPS):
        parts = [[] for _ in range(6)]
        for group in range(elems // 8):
            index = turned[group * 8 : group * 8 + 8, :].astype(jnp.int32)
            low = index & (LANES - 1)
            high = index >> 7
            for c in range(6):
                parts[c].append(
                    lookup(
                        lambda k: jnp.broadcast_to(
                            waves[c : c + 1, k * LANES : (k + 1) * LANES], (8, LANES)
                        ),
                        index,
                        low,
                        high,
                    )
                )
        values = jnp.concatenate([piece for part in parts for piece in part], 0)
        grads = jnp.dot(values, ahead[...], precision=TOP, preferred_element_type=f32)

        def grad(i, c):
            return grads[c * elems : (c + 1) * elems, i * LANES : (i + 1) * LANES]

        divs, devs = [], []
        for f in range(2):
            g = [[grad(i, f * 3 + j) for j in range(3)] for i in range(3)]
            div = g[0][0] + g[1][1] + g[2][2]
            third = div * (1.0 / 3.0)
            dev = {(i, i): g[i][i] - third for i in range(3)}
            for i, j in ((0, 1), (0, 2), (1, 2)):
                dev[i, j] = 0.5 * (g[i][j] + g[j][i])
            divs.append(div)
            devs.append(dev)
            pressure = kappa * div
            for (i, j), term in dev.items():
                tension = 2.0 * mu * term
                if i == j:
                    tension = tension + pressure
                for one, two in {(i, j), (j, i)}:
                    c = f * 3 + two
                    stress_buf[c * elems : (c + 1) * elems, one * LANES : (one + 1) * LANES] = (
                        tension
                    )
        bulk = bulk - KERNEL_WEIGHT * kappa * divs[0] * divs[1]
        both = {key: devs[0][key] * devs[1][key] for key in devs[0]}
        product = both[0, 0] + both[1, 1] + both[2, 2]
        product = product + 2.0 * (both[0, 1] + both[0, 2] + both[1, 2])
        shear = shear - 2.0 * KERNEL_WEIGHT * mu * product

        force_buf[0 : 6 * elems, :] = jnp.dot(
            stress_buf[...], back[...], precision=TOP, preferred_element_type=f32
        )
        for e in range(elems):
            place(
                e,
                force_buf[pl.ds(e, 8, stride=elems), :],
                turned[e : e + 1, :].astype(jnp.int32),
            )
        injected = jnp.concatenate(
            [jnp.zeros((3, LANES), f32), source[0, step], jnp.zeros((2, LANES), f32)], 0
        )
        place(elems, injected, rows[0:1, :])
        total = deposit(0, elems + 1)
        for k in range(slabs):
            forces[:, k * WIDE : (k + 1) * WIDE] = total[8 * k : 8 * k + 8]

        for which in range(2):
            for k in range(face_chunks):
                at = 1 + which * face_chunks + k
                index = jnp.broadcast_to(rows[at : at + 1, :], (8, LANES))
                face_send[step, which, :, k * LANES : (k + 1) * LANES] = lookup(
                    lambda q: forces[:, q * LANES : (q + 1) * LANES],
                    index,
                    index & (LANES - 1),
                    index >> 7,
                )
        if step == 0:
            pl.semaphore_wait(barrier, 2 + n_event - 1)
        copies = []
        for which, other in ((0, previous), (1, following)):
            copy = pltpu.make_async_remote_copy(
                src_ref=face_send.at[step, which],
                dst_ref=face_recv.at[step, 1 - which],
                send_sem=face_ssem.at[step, which],
                recv_sem=face_rsem.at[step, 1 - which],
                device_id={"mesh": other, "event": my_event},
                device_id_type=MESH,
            )
            copy.start()
            copies.append(copy)

        if step == STEPS - 1:
            for owner in range(n_event):
                kern_send[owner, 0] = bulk[owner * cols : (owner + 1) * cols]
                kern_send[owner, 1] = shear[owner * cols : (owner + 1) * cols]
            for hop in range(1, n_event):
                peer = lax.rem(my_event + hop, n_event)
                copy = pltpu.make_async_remote_copy(
                    src_ref=kern_send.at[peer],
                    dst_ref=kern_recv.at[hop - 1],
                    send_sem=kern_ssem.at[hop - 1],
                    recv_sem=kern_rsem.at[hop - 1],
                    device_id={"mesh": me, "event": peer},
                    device_id_type=MESH,
                )
                copy.start()
                pending.append(copy)

        for copy in copies:
            copy.wait()
        for which, inside in ((0, me > 0), (1, me < n_mesh - 1)):
            for k in range(face_chunks):
                at = 1 + which * face_chunks + k
                arrived = face_recv[step, which, :, k * LANES : (k + 1) * LANES]
                arrived = jnp.where(inside, arrived, 0.0)
                place(elems + at, arrived, rows[at : at + 1, :])
        total = deposit(elems + 1, elems + 1 + 2 * face_chunks)
        for k in range(slabs):
            span = slice(k * WIDE, (k + 1) * WIDE)
            assembled = forces[:, span] + total[8 * k : 8 * k + 8]
            now = waves[:, span]
            later = 2.0 * now - before[:, span] + scale_all[:, span] * assembled
            before[:, span] = now
            waves[:, span] = later

    fwd_out[0] = waves[0:3, 0:points]
    adj_out[0] = waves[3:6, 0:points]
    owned = kern_send[my_event]
    for copy in pending:
        copy.wait()
    for hop in range(1, n_event):
        owned = owned + kern_recv[hop - 1]
    for kind in range(2):
        block = jnp.concatenate(
            [owned[kind], jnp.zeros((LANES - cols, LANES), f32)], 0
        )
        kern_out[kind] = block.T[0:125, 0:cols]


def shards(
    n_mesh,
    n_event,
    forward_now,
    forward_prev,
    adjoint_now,
    adjoint_prev,
    connectivity,
    lower_face,
    upper_face,
    bulk_modulus,
    shear_modulus,
    step_scale,
    receiver_points,
    adjoint_source,
):
    points = forward_now.shape[2]
    face = lower_face.shape[1]
    elems = connectivity.shape[1]
    cols = elems // n_event
    slabs = -(-points // WIDE)
    slabs += slabs % 2
    width = slabs * WIDE
    face_chunks = -(-face // LANES)
    blocks = elems + 1 + 2 * face_chunks
    f32 = jnp.float32
    ahead, back = cube_tables()
    vmem = pl.BlockSpec(memory_space=pltpu.VMEM)
    call = pl.pallas_call(
        functools.partial(body, n_mesh, n_event, points, face, elems),
        out_shape=(
            jax.ShapeDtypeStruct(forward_now.shape, f32),
            jax.ShapeDtypeStruct(adjoint_now.shape, f32),
            jax.ShapeDtypeStruct((2, 125, cols), f32),
        ),
        in_specs=[vmem] * 14,
        out_specs=[vmem] * 3,
        scratch_shapes=[
            pltpu.VMEM((8, width), f32),
            pltpu.VMEM((8, width), f32),
            pltpu.VMEM((8, width), f32),
            pltpu.VMEM((8, width), f32),
            pltpu.VMEM((LANES, LANES), f32),
            pltpu.VMEM((LANES, LANES), f32),
            pltpu.VMEM((LANES, LANES), jnp.int32),
            pltpu.VMEM((LANES, LANES), jnp.int32),
            pltpu.VMEM((blocks * LANES, WIDE), jnp.bfloat16),
            pltpu.VMEM((3 * slabs * 8, blocks * LANES), jnp.bfloat16),
            pltpu.VMEM((6 * elems, 3 * LANES), f32),
            pltpu.VMEM((8 * elems, LANES), f32),
            pltpu.VMEM((STEPS, 2, 8, face_chunks * LANES), f32),
            pltpu.VMEM((STEPS, 2, 8, face_chunks * LANES), f32),
            pltpu.VMEM((n_event, 2, cols, LANES), f32),
            pltpu.VMEM((max(n_event - 1, 1), 2, cols, LANES), f32),
            pltpu.SemaphoreType.DMA((STEPS, 2)),
            pltpu.SemaphoreType.DMA((STEPS, 2)),
            pltpu.SemaphoreType.DMA((max(n_event - 1, 1),)),
            pltpu.SemaphoreType.DMA((max(n_event - 1, 1),)),
        ],
        compiler_params=pltpu.CompilerParams(
            collective_id=0, has_side_effects=True, vmem_limit_bytes=48 * 1024 * 1024
        ),
    )
    return call(
        forward_now,
        forward_prev,
        adjoint_now,
        adjoint_prev,
        connectivity,
        lower_face,
        upper_face,
        bulk_modulus,
        shear_modulus,
        step_scale.reshape(1, -1),
        receiver_points.reshape(1, -1),
        adjoint_source,
        jnp.asarray(ahead),
        jnp.asarray(back),
    )


def solution(mesh):
    placed = (
        P("event", None, "mesh"),
        P("event", None, "mesh"),
        P("event", None, "mesh"),
        P("event", None, "mesh"),
        P(None, "mesh"),
        P("mesh", None),
        P("mesh", None),
        P(None, "mesh"),
        P(None, "mesh"),
        P("mesh"),
        P("mesh"),
        P("event", None, None, "mesh"),
    )
    return jax.shard_map(
        functools.partial(shards, mesh.shape["mesh"], mesh.shape["event"]),
        mesh=mesh,
        in_specs=placed,
        out_specs=(
            P("event", None, "mesh"),
            P("event", None, "mesh"),
            P(None, None, ("mesh", "event")),
        ),
        check_vma=False,
    )
```

profile of v0, /device:TPU:0, one launch (start us, length us, event | category | flops | bytes accessed | tf_op | source)
XLA Modules:
  0.0 26.2 jit_solution(9671853200898074583)
XLA Ops:
  0.6 0.7 %copy.24.source = f32[1,2,3,128]{3,2,1,0:T(4,128)S(1)} copy(f32[1,2,3,128]{3,1,2,0:T(2,128)} %param.25) | data formatting | bytes 6144 | tf_op args[11]
  1.3 0.7 %reshape.12.scale = f32[1,2601]{1,0:T(1,128)S(1)} reshape(f32[2601]{0:T(1024)} %param.23) | data formatting | bytes 20808 | tf_op jit(solution)/shard_map/reshape | solution.py:398
  2.0 0.0 copy-start.5
  2.0 0.0 copy-start.8
  2.1 0.0 copy-start.9
  2.1 0.0 copy-start.10
  2.1 0.8 %copy.17.fwd_now = f32[1,3,2601]{2,1,0:T(4,128)S(1)} copy(f32[1,3,2601]{2,0,1:T(1,128)} %param.14) | data formatting | bytes 62424 | tf_op args[0]
  2.9 0.0 copy-done.5
  2.9 0.0 copy-start.6
  2.9 0.0 copy-start.7
  2.9 0.0 copy-start.4
  2.9 0.7 %copy-done.6 = f32[1,3,2601]{2,0,1:T(1,128)S(1)} copy-done((f32[1,3,2601]{2,0,1:T(1,128)S(1)}, f32[1,3,2601]{2,0,1:T(1,128)}, u32[]{:S(2)}) %copy-start.6) | copy-done | bytes 31236
  3.6 0.0 copy-start
  3.6 0.0 copy-start.1
  3.7 0.0 copy-done.7
  3.7 0.0 copy-done.8
  3.7 0.1 copy.21.conn
  3.8 0.0 copy-done.9
  3.8 0.1 copy.22.bulk_mod
  3.9 0.0 copy-done.10
  3.9 0.0 copy-start.2
  3.9 0.0 copy-start.3
  3.9 0.1 copy.23.shear_mod
  4.1 0.0 copy-done.4
  4.1 0.5 %copy-done = f32[384,128]{1,0:T(8,128)S(1)} copy-done((f32[384,128]{1,0:T(8,128)S(1)}, f32[384,128]{1,0:T(8,128)}, u32[]{:S(2)}) %copy-start) | copy-done | bytes 196632
  4.6 0.1 copy-done.1
  4.7 0.0 copy-done.2
  4.7 0.0 copy-done.3
  4.7 19.6 %shard_map.157 = (f32[1,3,2601]{2,1,0:T(4,128)S(1)}, f32[1,3,2601]{2,1,0:T(4,128)S(1)}, f32[2,125,8]{2,1,0:T(8,128)S(1)}) custom-call(f32[1,3,2601]{2,1,0:T(4,128)S(1)} %copy.17.fwd_now, f32[1,3,2601]{2,1,0:T(4,128)S(1)} %copy.18.fwd_prev, f32[1,3,2601]{2,1,0:T(4,128)S(1)} %copy.19.adj_now, f32[1,3,2601]{2,1,0:T(4,128)S(1)} %copy.20.adj_prev, ...), custom_call_target="tpu_custom_call" | custom-call | tf_op jit(solution)/shard_map/pallas_call | solution.py:388
  24.3 0.6 %copy.25 = f32[1,3,2601]{2,0,1:T(1,128)} copy(f32[1,3,2601]{2,1,0:T(4,128)S(1)} %get-tuple-element.3) | data formatting | bytes 62424 | tf_op jit(solution)/shard_map/pallas_call | solution.py:388
  24.9 0.7 %copy.27 = f32[2,125,8]{1,2,0:T(8,128)} copy(f32[2,125,8]{2,1,0:T(8,128)S(1)} %get-tuple-element.5) | data formatting | bytes 16000 | tf_op jit(solution)/shard_map/pallas_call | solution.py:388
  25.6 0.6 %copy.26 = f32[1,3,2601]{2,0,1:T(1,128)} copy(f32[1,3,2601]{2,1,0:T(4,128)S(1)} %get-tuple-element.4) | data formatting | bytes 62424 | tf_op jit(solution)/shard_map/pallas_call | solution.py:388
  (3 shorter events, 0.0 us)
Async XLA Ops:
  2.0 0.8 %copy-start.5 = (f32[1,3,2601]{2,0,1:T(1,128)S(1)}, f32[1,3,2601]{2,0,1:T(1,128)}, u32[]{:S(2)}) copy-start(f32[1,3,2601]{2,0,1:T(1,128)} %param.15) | copy-start | bytes 93640
  2.0 1.6 %copy-start.8 = (s32[125,32]{0,1:T(8,128)S(1)}, s32[125,32]{0,1:T(8,128)}, u32[]{:S(2)}) copy-start(s32[125,32]{0,1:T(8,128)} %param.18) | copy-start | bytes 48004
  2.1 1.8 %copy-start.9 = (f32[125,32]{0,1:T(8,128)S(1)}, f32[125,32]{0,1:T(8,128)}, u32[]{:S(2)}) copy-start(f32[125,32]{0,1:T(8,128)} %param.21) | copy-start | bytes 48004
  2.1 1.9 %copy-start.10 = (f32[125,32]{0,1:T(8,128)S(1)}, f32[125,32]{0,1:T(8,128)}, u32[]{:S(2)}) copy-start(f32[125,32]{0,1:T(8,128)} %param.22) | copy-start | bytes 48004
  2.9 0.8 %copy-start.6 = (f32[1,3,2601]{2,0,1:T(1,128)S(1)}, f32[1,3,2601]{2,0,1:T(1,128)}, u32[]{:S(2)}) copy-start(f32[1,3,2601]{2,0,1:T(1,128)} %param.16) | copy-start | bytes 93640
  2.9 0.8 %copy-start.7 = (f32[1,3,2601]{2,0,1:T(1,128)S(1)}, f32[1,3,2601]{2,0,1:T(1,128)}, u32[]{:S(2)}) copy-start(f32[1,3,2601]{2,0,1:T(1,128)} %param.17) | copy-start | bytes 93640
  2.9 1.2 %copy-start.4 = (s32[128]{0:T(128)S(1)}, s32[128]{0:T(128)}, u32[]{:S(2)}) copy-start(s32[128]{0:T(128)} %param.24) | copy-start | bytes 1540
  3.6 0.9 %copy-start = (f32[384,128]{1,0:T(8,128)S(1)}, f32[384,128]{1,0:T(8,128)}, u32[]{:S(2)}) copy-start(f32[384,128]{1,0:T(8,128)} %constant.5.clone.back) | copy-start | bytes 589828
  3.6 1.0 %copy-start.1 = (f32[128,384]{1,0:T(8,128)S(1)}, f32[128,384]{1,0:T(8,128)}, u32[]{:S(2)}) copy-start(f32[128,384]{1,0:T(8,128)} %constant.4.clone.ahead) | copy-start | bytes 589828
  3.9 0.7 %copy-start.2 = (s32[1,289]{1,0:T(1,128)S(1)}, s32[1,289]{1,0:T(1,128)}, u32[]{:S(2)}) copy-start(s32[1,289]{1,0:T(1,128)} %lower.1) | copy-start | bytes 3472
  3.9 0.7 %copy-start.3 = (s32[1,289]{1,0:T(1,128)S(1)}, s32[1,289]{1,0:T(1,128)}, u32[]{:S(2)}) copy-start(s32[1,289]{1,0:T(1,128)} %upper.1) | copy-start | bytes 3472
where the time goes:
time: 26.6 us; the launch traced here: 26.2 us
  Pallas kernels  19.6 us (74%)
  local copies, waits for them, and re-layouts  5.87 us (22%)
  between operations  0.77 us (3%)
    pallas_call x1, Pallas kernels, shards(): call(forward_now, forward_prev, adjoint_now, adjoint_prev, connectivity,...  19.6 us
    unnamed x30, local copies, waits for them, and re-layouts  3.19 us
    pallas_call x3, local copies, waits for them, and re-layouts, shards(): call(forward_now, forward_prev, adjoint_now, adjoint_prev, connectivity,...  1.96 us
    reshape x1, local copies, waits for them, and re-layouts, shards(): step_scale.reshape(1, -1)  0.71 us

commit v1 on v0

v1 whole, which is shorter than its diff:
```python
import functools
import math

import jax
import jax.numpy as jnp
import numpy as np
from jax import lax
from jax.experimental import pallas as pl
from jax.experimental.pallas import tpu as pltpu
from jax.sharding import PartitionSpec as P

STEPS = 2
LANES = 128
WIDE = 256
KERNEL_WEIGHT = 0.02
MESH = pl.DeviceIdType.MESH


def derivative_table():
    root = math.sqrt(3.0 / 7.0)
    points = [-1.0, -root, 0.0, root, 1.0]
    legendre = [(35.0 * x**4 - 30.0 * x**2 + 3.0) / 8.0 for x in points]
    table = np.zeros((5, 5))
    for row in range(5):
        for column in range(5):
            if row != column:
                table[row, column] = (
                    legendre[row] / legendre[column] / (points[row] - points[column])
                )
    table[0, 0] = -2.5
    table[4, 4] = 2.5
    return table


def cube_tables():
    deriv = derivative_table()
    line = np.array([0.1, 49.0 / 90.0, 32.0 / 45.0, 49.0 / 90.0, 0.1])
    cube = (line[:, None, None] * line[None, :, None] * line[None, None, :]).reshape(125)
    along = [
        np.kron(np.eye(25), deriv),
        np.kron(np.eye(5), np.kron(deriv, np.eye(5))),
        np.kron(deriv, np.eye(25)),
    ]
    ahead = np.zeros((LANES, 3 * LANES))
    back = np.zeros((3 * LANES, LANES))
    for i in range(3):
        ahead[:125, i * LANES : i * LANES + 125] = along[i].T
        back[i * LANES : i * LANES + 125, :125] = -along[i] * cube[:, None]
    return stacked(ahead), stacked(back)


def stacked(table):
    rest = table.astype(np.float32)
    parts = []
    for _ in range(3):
        part = rest.astype(jnp.bfloat16)
        rest = rest - part.astype(np.float32)
        parts.append(part)
    first, second, third = parts
    return np.concatenate([first, first, second, second, first, third], 0)


def three_parts(value):
    first = value.astype(jnp.bfloat16)
    rest = value - first.astype(jnp.float32)
    second = rest.astype(jnp.bfloat16)
    third = (rest - second.astype(jnp.float32)).astype(jnp.bfloat16)
    return first, second, third


def product(value, table):
    first, second, third = three_parts(value)
    wide = jnp.concatenate([first, second, first, second, third, first], 1)
    return jnp.dot(wide, table, preferred_element_type=jnp.float32)


def body(n_mesh, n_event, points, face, elems, *refs):
    sources, refs = refs[:14], refs[14:]
    (fwd_out, adj_out, kern_out), refs = refs[:3], refs[3:]
    held, refs = refs[:14], refs[14:]
    (
        fwd_now,
        fwd_prev,
        adj_now,
        adj_prev,
        conn,
        lower,
        upper,
        bulk_mod,
        shear_mod,
        scale,
        receivers,
        source,
        ahead,
        back,
    ) = held
    (
        load_sem,
        waves,
        before,
        later,
        scale_all,
        forces,
        slots,
        kappa_buf,
        mu_buf,
        rows,
        onehot,
        left,
        stress_buf,
        force_buf,
        face_send,
        face_recv,
        kern_send,
        kern_recv,
        face_ssem,
        face_rsem,
        kern_ssem,
        kern_rsem,
    ) = refs
    loads = [
        pltpu.make_async_copy(src, dst, load_sem.at[i])
        for i, (src, dst) in enumerate(zip(sources, held))
    ]
    for i in (4, 5, 6, 10, 0, 2, 12, 7, 8, 13, 11, 1, 3, 9):
        loads[i].start()

    me = lax.axis_index("mesh")
    my_event = lax.axis_index("event")
    following = lax.rem(me + 1, n_mesh)
    previous = lax.rem(me + n_mesh - 1, n_mesh)
    barrier = pltpu.get_barrier_semaphore()
    for other in (following, previous):
        pl.semaphore_signal(
            barrier, inc=1, device_id={"mesh": other, "event": my_event}, device_id_type=MESH
        )
    for hop in range(1, n_event):
        peer = lax.rem(my_event + hop, n_event)
        pl.semaphore_signal(
            barrier, inc=1, device_id={"mesh": me, "event": peer}, device_id_type=MESH
        )

    f32 = jnp.float32
    bf16 = jnp.bfloat16
    chunks = -(-points // LANES)
    slabs = waves.shape[1] // WIDE
    face_chunks = face_send.shape[3] // LANES
    part_rows = left.shape[0] // 3
    cols = elems // n_event
    tile = (8, LANES)

    def lanes_of(k):
        return slice(k * LANES, (k + 1) * LANES)

    rows[...] = jnp.full(rows.shape, -1, jnp.int32)
    waves[...] = jnp.zeros_like(waves)
    before[...] = jnp.zeros_like(before)
    scale_all[...] = jnp.zeros_like(scale_all)
    kappa_buf[...] = jnp.zeros_like(kappa_buf)
    mu_buf[...] = jnp.zeros_like(mu_buf)
    force_buf[...] = jnp.zeros_like(force_buf)
    for i in (4, 5, 6, 10):
        loads[i].wait()
    rows[0:elems, 0:125] = conn[...]
    rows[elems : elems + 1, :] = receivers[...]
    for which, ref in enumerate((lower, upper)):
        for k in range(face_chunks):
            size = min(LANES, face - k * LANES)
            at = elems + 1 + which * face_chunks + k
            rows[at : at + 1, 0:size] = ref[:, k * LANES : k * LANES + size]
    columns = (rows[...].astype(f32).T.astype(jnp.int32) & (WIDE - 1)).astype(f32).astype(bf16)

    lane = lax.broadcasted_iota(jnp.int32, (LANES, WIDE), 1).astype(f32).astype(bf16)
    one = jnp.ones((LANES, WIDE), bf16)
    none = jnp.zeros((LANES, WIDE), bf16)
    half = lax.broadcasted_iota(jnp.int32, (16, LANES), 0) >> 3
    empty = jnp.zeros((16, LANES), bf16)

    def spread(at):
        low = jnp.broadcast_to(columns[:, at : at + 1], (LANES, WIDE))
        onehot[at * LANES : (at + 1) * LANES, :] = jnp.where(lane == low, one, none)

    def take(table, low):
        return jnp.take_along_axis(table, low, axis=1, mode="promise_in_bounds")

    def lookup(tables, index, count):
        low = index & (LANES - 1)
        high = index >> 7
        outs = [jnp.zeros(index.shape, f32) for _ in tables]
        for k in range(count):
            here = high == k
            for t, table in enumerate(tables):
                outs[t] = jnp.where(here, take(table(k), low), outs[t])
        return outs

    def row_of(ref, c):
        return lambda k: jnp.broadcast_to(ref[c : c + 1, lanes_of(k)], tile)

    def place(at, value):
        high = jnp.broadcast_to(rows[at : at + 1, :] >> 8, (16, LANES)) - half
        high = high.astype(f32).astype(bf16)
        parts = three_parts(jnp.concatenate([value, value], 0))
        for k in range(part_rows // 16):
            here = high == jnp.full((16, LANES), 2 * k, bf16)
            for s, part in enumerate(parts):
                row = s * part_rows + 16 * k
                left[row : row + 16, lanes_of(at)] = jnp.where(here, part, empty)

    def deposit(start, stop, out):
        span = slice(start * LANES, stop * LANES)
        total = jnp.dot(left[:, span], onehot[span, :], preferred_element_type=f32)
        total = total[0:part_rows] + total[part_rows : 2 * part_rows] + total[2 * part_rows :]
        for k in range(slabs):
            out[:, k * WIDE : (k + 1) * WIDE] = total[8 * k : 8 * k + 8]

    def element_index(group):
        return rows[group * 8 : group * 8 + 8, :]

    def at_elements(ref):
        parts = [[] for _ in range(6)]
        for group in range(elems // 8):
            got = lookup([row_of(ref, c) for c in range(6)], element_index(group), chunks)
            for c in range(6):
                parts[c].append(got[c])
        return parts

    for i in (0, 2):
        loads[i].wait()
    for c in range(3):
        waves[c : c + 1, 0:points] = fwd_now[c]
        waves[3 + c : 4 + c, 0:points] = adj_now[c]
    parts = at_elements(waves)
    for e in range(elems + 1):
        spread(e)
    for i in (12, 7, 8):
        loads[i].wait()
    kappa_buf[:, 0:125] = bulk_mod[...]
    mu_buf[:, 0:125] = shear_mod[...]
    kappa = kappa_buf[...]
    mu = mu_buf[...]

    span = ahead.shape[0] // 3
    forward_table = jnp.concatenate([ahead[i * span : (i + 1) * span, :] for i in range(3)], 1)
    bulk = jnp.zeros((elems, LANES), f32)
    shear = jnp.zeros((elems, LANES), f32)
    pending = []
    for step in range(STEPS):
        values = jnp.concatenate([piece for part in parts for piece in part], 0)
        grads = product(values, forward_table)

        def grad(i, c):
            return grads[c * elems : (c + 1) * elems, i * LANES : (i + 1) * LANES]

        divs, devs = [], []
        for f in range(2):
            g = [[grad(i, f * 3 + j) for j in range(3)] for i in range(3)]
            div = g[0][0] + g[1][1] + g[2][2]
            third = div * (1.0 / 3.0)
            dev = {(i, i): g[i][i] - third for i in range(3)}
            for i, j in ((0, 1), (0, 2), (1, 2)):
                dev[i, j] = 0.5 * (g[i][j] + g[j][i])
            divs.append(div)
            devs.append(dev)
            pressure = kappa * div
            for (i, j), term in dev.items():
                tension = 2.0 * mu * term
                if i == j:
                    tension = tension + pressure
                for first, second in ((i, j), (j, i))[: 1 + (i != j)]:
                    c = f * 3 + second
                    stress_buf[c * elems : (c + 1) * elems, lanes_of(first)] = tension

        if step == 0:
            loads[13].wait()
        force_buf[0 : 6 * elems, :] = product(stress_buf[...], back[...])
        for e in range(elems):
            place(e, force_buf[pl.ds(e, 8, stride=elems), :])
        if step == 0:
            loads[11].wait()
        injected = jnp.concatenate(
            [jnp.zeros((3, LANES), f32), source[0, :, step, :], jnp.zeros((2, LANES), f32)], 0
        )
        place(elems, injected)
        deposit(0, elems + 1, forces)

        copies = []
        if step == 0:
            pl.semaphore_wait(barrier, 2 + n_event - 1)
        for which, other in ((0, previous), (1, following)):
            for k in range(face_chunks):
                at = elems + 1 + which * face_chunks + k
                index = jnp.broadcast_to(rows[at : at + 1, :], tile)
                face_send[step, which, :, lanes_of(k)] = lookup(
                    [lambda q: forces[:, lanes_of(q)]], index, chunks
                )[0]
            copy = pltpu.make_async_remote_copy(
                src_ref=face_send.at[step, which],
                dst_ref=face_recv.at[step, 1 - which],
                send_sem=face_ssem.at[step, which],
                recv_sem=face_rsem.at[step, 1 - which],
                device_id={"mesh": other, "event": my_event},
                device_id_type=MESH,
            )
            copy.start()
            copies.append(copy)

        bulk = bulk - KERNEL_WEIGHT * kappa * divs[0] * divs[1]
        both = {key: devs[0][key] * devs[1][key] for key in devs[0]}
        paired = both[0, 0] + both[1, 1] + both[2, 2]
        paired = paired + 2.0 * (both[0, 1] + both[0, 2] + both[1, 2])
        shear = shear - 2.0 * KERNEL_WEIGHT * mu * paired

        if step == STEPS - 1:
            for owner in range(n_event):
                kern_send[owner, 0] = bulk[owner * cols : (owner + 1) * cols]
                kern_send[owner, 1] = shear[owner * cols : (owner + 1) * cols]
            for hop in range(1, n_event):
                peer = lax.rem(my_event + hop, n_event)
                copy = pltpu.make_async_remote_copy(
                    src_ref=kern_send.at[peer],
                    dst_ref=kern_recv.at[hop - 1],
                    send_sem=kern_ssem.at[hop - 1],
                    recv_sem=kern_rsem.at[hop - 1],
                    device_id={"mesh": me, "event": peer},
                    device_id_type=MESH,
                )
                copy.start()
                pending.append(copy)

        if step == 0:
            for i in (1, 3, 9):
                loads[i].wait()
            for c in range(3):
                before[c : c + 1, 0:points] = fwd_prev[c]
                before[3 + c : 4 + c, 0:points] = adj_prev[c]
            scale_all[:, 0:points] = jnp.broadcast_to(scale[...].reshape(1, points), (8, points))
            later[...] = 2.0 * waves[...] - before[...] + scale_all[...] * forces[...]
            parts = at_elements(later)
            number = lax.broadcasted_iota(jnp.int32, tile, 1)
            for which, inside in ((0, me > 0), (1, me < n_mesh - 1)):
                for k in range(face_chunks):
                    at = elems + 1 + which * face_chunks + k
                    spread(at)
                    slot = number + ((which * face_chunks + k) * LANES + 1)
                    place(at, jnp.where(inside, slot.astype(f32), 0.0))
            deposit(elems + 1, elems + 1 + 2 * face_chunks, slots)
            extras = [
                lookup([row_of(scale_all, 0), row_of(slots, 0)], element_index(group), chunks)
                for group in range(elems // 8)
            ]
            for copy in copies:
                copy.wait()
            for group in range(elems // 8):
                which = 0 if group < elems // 16 else 1
                factor, slot = extras[group]
                index = slot.astype(jnp.int32) - (1 + which * face_chunks * LANES)
                got = lookup(
                    [row_of(face_recv.at[step, which], c) for c in range(6)], index, face_chunks
                )
                for c in range(6):
                    parts[c][group] = parts[c][group] + factor * got[c]
        else:

            def arrived(at, q):
                index = slots[:, lanes_of(q)].astype(jnp.int32) - 1
                return lookup(
                    [
                        lambda k: face_recv[
                            at, k // face_chunks, :, lanes_of(k % face_chunks)
                        ]
                    ],
                    index,
                    2 * face_chunks,
                )[0]

            for q in range(chunks):
                span = lanes_of(q)
                now = later[:, span] + scale_all[:, span] * arrived(0, q)
                before[:, span] = (
                    2.0 * now - waves[:, span] + scale_all[:, span] * forces[:, span]
                )
            for copy in copies:
                copy.wait()
            for q in range(chunks):
                span = lanes_of(q)
                later[:, span] = before[:, span] + scale_all[:, span] * arrived(1, q)

    for c in range(3):
        fwd_out[c] = later[c : c + 1, 0:points]
        adj_out[c] = later[3 + c : 4 + c, 0:points]
    owned = kern_send[my_event]
    for copy in pending:
        copy.wait()
    for hop in range(1, n_event):
        owned = owned + kern_recv[hop - 1]
    kern_out[...] = owned[:, :, 0:125]


def shards(
    n_mesh,
    n_event,
    forward_now,
    forward_prev,
    adjoint_now,
    adjoint_prev,
    connectivity,
    lower_face,
    upper_face,
    bulk_modulus,
    shear_modulus,
    step_scale,
    receiver_points,
    adjoint_source,
):
    points = forward_now.shape[2]
    face = lower_face.shape[1]
    elems = connectivity.shape[1]
    cols = elems // n_event
    slabs = -(-points // WIDE)
    slabs += slabs % 2
    width = slabs * WIDE
    face_chunks = -(-face // LANES)
    blocks = elems + 1 + 2 * face_chunks
    f32 = jnp.float32
    ahead, back = cube_tables()
    fields = [v.transpose(1, 0, 2) for v in (forward_now, forward_prev, adjoint_now, adjoint_prev)]
    operands = (
        *fields,
        connectivity.T,
        lower_face,
        upper_face,
        bulk_modulus.T,
        shear_modulus.T,
        step_scale,
        receiver_points.reshape(1, -1),
        adjoint_source.transpose(0, 2, 1, 3),
        jnp.asarray(np.concatenate(np.split(ahead, 3, 1), 0)),
        jnp.asarray(back),
    )
    state = pltpu.VMEM((8, width), f32)
    moduli = pltpu.VMEM((elems, LANES), f32)
    peers = max(n_event - 1, 1)
    call = pl.pallas_call(
        functools.partial(body, n_mesh, n_event, points, face, elems),
        out_shape=(
            jax.ShapeDtypeStruct(fields[0].shape, f32),
            jax.ShapeDtypeStruct(fields[2].shape, f32),
            jax.ShapeDtypeStruct((2, cols, 125), f32),
        ),
        in_specs=[pl.BlockSpec(memory_space=pl.ANY)] * 14,
        out_specs=[pl.BlockSpec(memory_space=pltpu.VMEM)] * 3,
        scratch_shapes=[
            *[pltpu.VMEM(v.shape, v.dtype) for v in operands],
            pltpu.SemaphoreType.DMA((14,)),
            state,
            state,
            state,
            state,
            state,
            state,
            moduli,
            moduli,
            pltpu.VMEM((LANES, LANES), jnp.int32),
            pltpu.VMEM((blocks * LANES, WIDE), jnp.bfloat16),
            pltpu.VMEM((3 * slabs * 8, blocks * LANES), jnp.bfloat16),
            pltpu.VMEM((6 * elems, 3 * LANES), f32),
            pltpu.VMEM((8 * elems, LANES), f32),
            pltpu.VMEM((STEPS, 2, 8, face_chunks * LANES), f32),
            pltpu.VMEM((STEPS, 2, 8, face_chunks * LANES), f32),
            pltpu.VMEM((n_event, 2, cols, LANES), f32),
            pltpu.VMEM((peers, 2, cols, LANES), f32),
            pltpu.SemaphoreType.DMA((STEPS, 2)),
            pltpu.SemaphoreType.DMA((STEPS, 2)),
            pltpu.SemaphoreType.DMA((peers,)),
            pltpu.SemaphoreType.DMA((peers,)),
        ],
        compiler_params=pltpu.CompilerParams(
            collective_id=0, has_side_effects=True, vmem_limit_bytes=63 * 1024 * 1024
        ),
    )
    forward, adjoint, kernels = call(*operands)
    return (forward.transpose(1, 0, 2), adjoint.transpose(1, 0, 2), kernels.transpose(0, 2, 1))


def solution(mesh):
    placed = (
        P("event", None, "mesh"),
        P("event", None, "mesh"),
        P("event", None, "mesh"),
        P("event", None, "mesh"),
        P(None, "mesh"),
        P("mesh", None),
        P("mesh", None),
        P(None, "mesh"),
        P(None, "mesh"),
        P("mesh"),
        P("mesh"),
        P("event", None, None, "mesh"),
    )
    return jax.shard_map(
        functools.partial(shards, mesh.shape["mesh"], mesh.shape["event"]),
        mesh=mesh,
        in_specs=placed,
        out_specs=(
            P("event", None, "mesh"),
            P("event", None, "mesh"),
            P(None, None, ("mesh", "event")),
        ),
        check_vma=False,
    )
```

time: 26.6 us -> 21.9 us (0.82)
  local copies, waits for them, and re-layouts: 5.87 us -> 2.69 us
  Pallas kernels: 19.6 us -> 18.3 us
    pallas_call x3 -> x0, local copies, waits for them, and re-layouts: 1.96 us -> none  [shards(): call(forward_now, forward_prev, adjoint_now, adjoint_prev, connectivity,...]
    pallas_call x1, Pallas kernels: 19.6 us -> 18.3 us  [shards(): forward, adjoint, kernels = call(*operands)]
    reshape x1 -> x0, local copies, waits for them, and re-layouts: 0.71 us -> none  [shards(): step_scale.reshape(1, -1)]
    unnamed x30 -> x7, local copies, waits for them, and re-layouts: 3.19 us -> 2.69 us
where the time goes in v1:
time: 21.9 us; the launch traced here: 21.6 us
  Pallas kernels  18.3 us (84%)
  local copies, waits for them, and re-layouts  2.69 us (12%)
  between operations  0.65 us (3%)
    pallas_call x1, Pallas kernels, shards(): forward, adjoint, kernels = call(*operands)  18.3 us
    unnamed x7, local copies, waits for them, and re-layouts  2.69 us

profile of v1, /device:TPU:0, one launch (start us, length us, event | category | flops | bytes accessed | tf_op | source)
XLA Modules:
  0.0 21.6 jit_solution(12094282639396975824)
XLA Ops:
  0.6 18.3 %shard_map.157 = (f32[3,1,2601]{2,1,0:T(1,128)}, f32[3,1,2601]{2,1,0:T(1,128)}, f32[2,8,125]{2,1,0:T(8,128)}) custom-call(f32[3,1,2601]{2,1,0:T(1,128)} %bitcast.12, f32[3,1,2601]{2,1,0:T(1,128)} %bitcast.13, f32[3,1,2601]{2,1,0:T(1,128)} %bitcast.14, f32[3,1,2601]{2,1,0:T(1,128)} %bitcast.15, s32[32,125]{1,0:T(8,128)} %bitcast.18, s32[1,289]{1,0:T(1,128)} %refs_5_.1, ...), custom_call_target="tpu_custom_call" | custom-call | tf_op jit(solution)/shard_map/pallas_call | solution.py:481
  18.9 0.0 copy-start
  18.9 1.4 %copy.20 = f32[1,3,2601]{2,0,1:T(1,128)} copy(f32[1,3,2601]{2,0,1:T(1,128)} %bitcast.17) | data formatting | bytes 62424
  20.3 0.0 copy-done
  20.3 0.0 copy-start.1
  20.3 0.6 %copy.21 = f32[1,3,2601]{2,0,1:T(1,128)} copy(f32[1,3,2601]{2,0,1:T(1,128)S(1)} %bitcast.16) | data formatting | bytes 62424
  20.9 0.1 copy-done.1
  21.0 0.6 %copy.22 = f32[2,125,8]{1,2,0:T(8,128)} copy(f32[2,125,8]{1,2,0:T(8,128)S(1)} %bitcast.21) | data formatting | bytes 16000
Async XLA Ops:
  18.9 1.4 %copy-start = (f32[3,1,2601]{2,1,0:T(1,128)S(1)}, f32[3,1,2601]{2,1,0:T(1,128)}, u32[]{:S(2)}) copy-start(f32[3,1,2601]{2,1,0:T(1,128)} %get-tuple-element.7) | copy-start | bytes 93640
  20.3 0.7 %copy-start.1 = (f32[2,8,125]{2,1,0:T(8,128)S(1)}, f32[2,8,125]{2,1,0:T(8,128)}, u32[]{:S(2)}) copy-start(f32[2,8,125]{2,1,0:T(8,128)} %get-tuple-element.8) | copy-start | bytes 24004

commit v2 on v1

--- a/solution.py
+++ b/solution.py
@@ -52,25 +52,23 @@
 def stacked(table):
     rest = table.astype(np.float32)
     parts = []
-    for _ in range(3):
+    for _ in range(2):
         part = rest.astype(jnp.bfloat16)
         rest = rest - part.astype(np.float32)
         parts.append(part)
-    first, second, third = parts
-    return np.concatenate([first, first, second, second, first, third], 0)
-
-
-def three_parts(value):
+    first, second = parts
+    return np.concatenate([first, first, second, second], 0)
+
+
+def two_parts(value):
     first = value.astype(jnp.bfloat16)
-    rest = value - first.astype(jnp.float32)
-    second = rest.astype(jnp.bfloat16)
-    third = (rest - second.astype(jnp.float32)).astype(jnp.bfloat16)
-    return first, second, third
+    second = (value - first.astype(jnp.float32)).astype(jnp.bfloat16)
+    return first, second
 
 
 def product(value, table):
-    first, second, third = three_parts(value)
-    wide = jnp.concatenate([first, second, first, second, third, first], 1)
+    first, second = two_parts(value)
+    wide = jnp.concatenate([first, second, first, second], 1)
     return jnp.dot(wide, table, preferred_element_type=jnp.float32)
 
 
@@ -145,7 +143,7 @@
     chunks = -(-points // LANES)
     slabs = waves.shape[1] // WIDE
     face_chunks = face_send.shape[3] // LANES
-    part_rows = left.shape[0] // 3
+    part_rows = left.shape[0] // 2
     cols = elems // n_event
     tile = (8, LANES)
 
@@ -199,7 +197,7 @@
     def place(at, value):
         high = jnp.broadcast_to(rows[at : at + 1, :] >> 8, (16, LANES)) - half
         high = high.astype(f32).astype(bf16)
-        parts = three_parts(jnp.concatenate([value, value], 0))
+        parts = two_parts(jnp.concatenate([value, value], 0))
         for k in range(part_rows // 16):
             here = high == jnp.full((16, LANES), 2 * k, bf16)
             for s, part in enumerate(parts):
@@ -209,7 +207,7 @@
     def deposit(start, stop, out):
         span = slice(start * LANES, stop * LANES)
         total = jnp.dot(left[:, span], onehot[span, :], preferred_element_type=f32)
-        total = total[0:part_rows] + total[part_rows : 2 * part_rows] + total[2 * part_rows :]
+        total = total[0:part_rows] + total[part_rows:]
         for k in range(slabs):
             out[:, k * WIDE : (k + 1) * WIDE] = total[8 * k : 8 * k + 8]
 
@@ -394,6 +392,28 @@
     for hop in range(1, n_event):
         owned = owned + kern_recv[hop - 1]
     kern_out[...] = owned[:, :, 0:125]
+
+
+def copy_out(*refs):
+    count = len(refs) // 2
+    sem = refs[-1]
+    copies = [pltpu.make_async_copy(refs[i], refs[count + i], sem.at[i]) for i in range(count)]
+    for copy in copies:
+        copy.start()
+    for copy in copies:
+        copy.wait()
+
+
+def hand_out(results):
+    count = len(results)
+    return pl.pallas_call(
+        copy_out,
+        out_shape=tuple(jax.ShapeDtypeStruct(v.shape, v.dtype) for v in results),
+        in_specs=[pl.BlockSpec(memory_space=pltpu.HBM)] * count,
+        out_specs=[pl.BlockSpec(memory_space=pltpu.HBM)] * count,
+        scratch_shapes=[pltpu.SemaphoreType.DMA((count,))],
+        compiler_params=pltpu.CompilerParams(vmem_limit_bytes=60 * 1024 * 1024),
+    )(*results)
 
 
 def shards(
@@ -447,7 +467,7 @@
             jax.ShapeDtypeStruct(fields[2].shape, f32),
             jax.ShapeDtypeStruct((2, cols, 125), f32),
         ),
-        in_specs=[pl.BlockSpec(memory_space=pl.ANY)] * 14,
+        in_specs=[pl.BlockSpec(memory_space=pltpu.HBM)] * 14,
         out_specs=[pl.BlockSpec(memory_space=pltpu.VMEM)] * 3,
         scratch_shapes=[
             *[pltpu.VMEM(v.shape, v.dtype) for v in operands],
@@ -462,7 +482,7 @@
             moduli,
             pltpu.VMEM((LANES, LANES), jnp.int32),
             pltpu.VMEM((blocks * LANES, WIDE), jnp.bfloat16),
-            pltpu.VMEM((3 * slabs * 8, blocks * LANES), jnp.bfloat16),
+            pltpu.VMEM((2 * slabs * 8, blocks * LANES), jnp.bfloat16),
             pltpu.VMEM((6 * elems, 3 * LANES), f32),
             pltpu.VMEM((8 * elems, LANES), f32),
             pltpu.VMEM((STEPS, 2, 8, face_chunks * LANES), f32),
@@ -475,10 +495,10 @@
             pltpu.SemaphoreType.DMA((peers,)),
         ],
         compiler_params=pltpu.CompilerParams(
-            collective_id=0, has_side_effects=True, vmem_limit_bytes=63 * 1024 * 1024
+            collective_id=0, has_side_effects=True, vmem_limit_bytes=60 * 1024 * 1024
         ),
     )
-    forward, adjoint, kernels = call(*operands)
+    forward, adjoint, kernels = hand_out(call(*operands))
     return (forward.transpose(1, 0, 2), adjoint.transpose(1, 0, 2), kernels.transpose(0, 2, 1))
 
 

time: 21.9 us -> 21.5 us (0.982)
  local copies, waits for them, and re-layouts: 2.69 us -> 0 us
  Pallas kernels: 18.3 us -> 20.6 us
    unnamed x7 -> x0, local copies, waits for them, and re-layouts: 2.69 us -> none
    pallas_call x1 -> x2, Pallas kernels: 18.3 us -> 20.6 us  [the longest x1 17.3 us: shards(): forward, adjoint, kernels = hand_out(call(*operands))]
where the time goes in v2:
time: 21.5 us; the launch traced here: 21.2 us
  Pallas kernels  20.6 us (96%)
  between operations  0.64 us (3%)
    pallas_call x1, Pallas kernels, shards(): forward, adjoint, kernels = hand_out(call(*operands))  17.3 us
    pallas_call x1, Pallas kernels, hand_out(): pl.pallas_call(copy_out, out_shape=tuple((jax.ShapeDtypeStruct(v.shape, v...  3.33 us

profile of v2, /device:TPU:0, one launch (start us, length us, event | category | flops | bytes accessed | tf_op | source)
XLA Modules:
  0.0 21.2 jit_solution(7128310579658124010)
XLA Ops:
  0.6 17.3 %shard_map.157 = (f32[3,1,2601]{2,1,0:T(1,128)}, f32[3,1,2601]{2,1,0:T(1,128)}, f32[2,8,125]{2,1,0:T(8,128)}) custom-call(f32[3,1,2601]{2,1,0:T(1,128)} %bitcast.12, f32[3,1,2601]{2,1,0:T(1,128)} %bitcast.13, f32[3,1,2601]{2,1,0:T(1,128)} %bitcast.14, f32[3,1,2601]{2,1,0:T(1,128)} %bitcast.15, s32[32,125]{1,0:T(8,128)} %bitcast.16, s32[1,289]{1,0:T(1,128)} %refs_5_.1, ...), custom_call_target="tpu_custom_call" | custom-call | tf_op jit(solution)/shard_map/pallas_call | solution.py:501
  17.9 3.3 %shard_map.158 = (f32[3,1,2601]{2,1,0:T(1,128)}, f32[3,1,2601]{2,1,0:T(1,128)}, f32[2,8,125]{2,1,0:T(8,128)}) custom-call(f32[3,1,2601]{2,1,0:T(1,128)} %get-tuple-element.9.refs_0_, f32[3,1,2601]{2,1,0:T(1,128)} %get-tuple-element.10.refs_1_, f32[2,8,125]{2,1,0:T(8,128)} %get-tuple-element.11.refs_2_), custom_call_target="tpu_custom_call" | custom-call | tf_op jit(solution)/shard_map/pallas_call | solution.py:409

commit v3 on v2

--- a/solution.py
+++ b/solution.py
@@ -409,10 +409,10 @@
     return pl.pallas_call(
         copy_out,
         out_shape=tuple(jax.ShapeDtypeStruct(v.shape, v.dtype) for v in results),
-        in_specs=[pl.BlockSpec(memory_space=pltpu.HBM)] * count,
+        in_specs=[pl.BlockSpec(memory_space=pltpu.VMEM)] * count,
         out_specs=[pl.BlockSpec(memory_space=pltpu.HBM)] * count,
         scratch_shapes=[pltpu.SemaphoreType.DMA((count,))],
-        compiler_params=pltpu.CompilerParams(vmem_limit_bytes=60 * 1024 * 1024),
+        compiler_params=pltpu.CompilerParams(vmem_limit_bytes=1024 * 1024),
     )(*results)
 
 
@@ -463,9 +463,9 @@
     call = pl.pallas_call(
         functools.partial(body, n_mesh, n_event, points, face, elems),
         out_shape=(
-            jax.ShapeDtypeStruct(fields[0].shape, f32),
-            jax.ShapeDtypeStruct(fields[2].shape, f32),
-            jax.ShapeDtypeStruct((2, cols, 125), f32),
+            pltpu.VMEM(fields[0].shape, f32),
+            pltpu.VMEM(fields[2].shape, f32),
+            pltpu.VMEM((2, cols, 125), f32),
         ),
         in_specs=[pl.BlockSpec(memory_space=pltpu.HBM)] * 14,
         out_specs=[pl.BlockSpec(memory_space=pltpu.VMEM)] * 3,

time: 21.5 us -> 18.2 us (0.85)
  Pallas kernels: 20.6 us -> 17.3 us
    pallas_call x1, Pallas kernels: 3.33 us -> 0.65 us  [hand_out(): pl.pallas_call(copy_out, out_shape=tuple((jax.ShapeDtypeStruct(v.shape, v...]
    pallas_call x1, Pallas kernels: 17.3 us -> 16.6 us  [shards(): forward, adjoint, kernels = hand_out(call(*operands))]
where the time goes in v3:
time: 18.2 us; the launch traced here: 17.9 us
  Pallas kernels  17.3 us (95%)
  between operations  0.64 us (4%)
    pallas_call x1, Pallas kernels, shards(): forward, adjoint, kernels = hand_out(call(*operands))  16.6 us
    pallas_call x1, Pallas kernels, hand_out(): pl.pallas_call(copy_out, out_shape=tuple((jax.ShapeDtypeStruct(v.shape, v...  0.65 us

profile of v3, /device:TPU:0, one launch (start us, length us, event | category | flops | bytes accessed | tf_op | source)
XLA Modules:
  0.0 17.9 jit_solution(7066643122865525260)
XLA Ops:
  0.6 16.6 %shard_map.157 = (f32[3,1,2601]{2,1,0:T(1,128)S(1)}, f32[3,1,2601]{2,1,0:T(1,128)S(1)}, f32[2,8,125]{2,1,0:T(8,128)S(1)}) custom-call(f32[3,1,2601]{2,1,0:T(1,128)} %bitcast.12, f32[3,1,2601]{2,1,0:T(1,128)} %bitcast.13, f32[3,1,2601]{2,1,0:T(1,128)} %bitcast.14, f32[3,1,2601]{2,1,0:T(1,128)} %bitcast.15, s32[32,125]{1,0:T(8,128)} %bitcast.16, ...), custom_call_target="tpu_custom_call" | custom-call | tf_op jit(solution)/shard_map/pallas_call | solution.py:501
  17.3 0.7 %shard_map.158 = (f32[3,1,2601]{2,1,0:T(1,128)}, f32[3,1,2601]{2,1,0:T(1,128)}, f32[2,8,125]{2,1,0:T(8,128)}) custom-call(f32[3,1,2601]{2,1,0:T(1,128)S(1)} %get-tuple-element.9.refs_0_, f32[3,1,2601]{2,1,0:T(1,128)S(1)} %get-tuple-element.10.refs_1_, f32[2,8,125]{2,1,0:T(8,128)S(1)} %get-tuple-element.11.refs_2_), custom_call_target="tpu_custom_call" | custom-call | tf_op jit(solution)/shard_map/pallas_call | solution.py:409

commit v4 on v3

--- a/solution.py
+++ b/solution.py
@@ -57,7 +57,7 @@
         rest = rest - part.astype(np.float32)
         parts.append(part)
     first, second = parts
-    return np.concatenate([first, first, second, second], 0)
+    return np.concatenate([first, first, second], 0)
 
 
 def two_parts(value):
@@ -68,7 +68,7 @@
 
 def product(value, table):
     first, second = two_parts(value)
-    wide = jnp.concatenate([first, second, first, second], 1)
+    wide = jnp.concatenate([first, second, first], 1)
     return jnp.dot(wide, table, preferred_element_type=jnp.float32)
 
 
@@ -109,6 +109,7 @@
         force_buf,
         face_send,
         face_recv,
+        face_scaled,
         kern_send,
         kern_recv,
         face_ssem,
@@ -222,7 +223,7 @@
                 parts[c].append(got[c])
         return parts
 
-    for i in (0, 2):
+    for i in (0, 2, 12, 7, 8, 13, 11, 1, 3, 9):
         loads[i].wait()
     for c in range(3):
         waves[c : c + 1, 0:points] = fwd_now[c]
@@ -230,8 +231,6 @@
     parts = at_elements(waves)
     for e in range(elems + 1):
         spread(e)
-    for i in (12, 7, 8):
-        loads[i].wait()
     kappa_buf[:, 0:125] = bulk_mod[...]
     mu_buf[:, 0:125] = shear_mod[...]
     kappa = kappa_buf[...]
@@ -268,13 +267,9 @@
                     c = f * 3 + second
                     stress_buf[c * elems : (c + 1) * elems, lanes_of(first)] = tension
 
-        if step == 0:
-            loads[13].wait()
         force_buf[0 : 6 * elems, :] = product(stress_buf[...], back[...])
         for e in range(elems):
             place(e, force_buf[pl.ds(e, 8, stride=elems), :])
-        if step == 0:
-            loads[11].wait()
         injected = jnp.concatenate(
             [jnp.zeros((3, LANES), f32), source[0, :, step, :], jnp.zeros((2, LANES), f32)], 0
         )
@@ -326,8 +321,6 @@
                 pending.append(copy)
 
         if step == 0:
-            for i in (1, 3, 9):
-                loads[i].wait()
             for c in range(3):
                 before[c : c + 1, 0:points] = fwd_prev[c]
                 before[3 + c : 4 + c, 0:points] = adj_prev[c]
@@ -342,21 +335,28 @@
                     slot = number + ((which * face_chunks + k) * LANES + 1)
                     place(at, jnp.where(inside, slot.astype(f32), 0.0))
             deposit(elems + 1, elems + 1 + 2 * face_chunks, slots)
-            extras = [
-                lookup([row_of(scale_all, 0), row_of(slots, 0)], element_index(group), chunks)
+            found = [
+                lookup([row_of(slots, 0)], element_index(group), chunks)[0]
                 for group in range(elems // 8)
             ]
+            factors = lookup([row_of(scale_all, 0)], rows[elems : elems + 8, :], chunks)[0]
             for copy in copies:
                 copy.wait()
+            for which in range(2):
+                for k in range(face_chunks):
+                    at = 1 + which * face_chunks + k
+                    span = lanes_of(k)
+                    face_scaled[which, :, span] = (
+                        face_recv[step, which, :, span] * factors[at : at + 1, :]
+                    )
             for group in range(elems // 8):
                 which = 0 if group < elems // 16 else 1
-                factor, slot = extras[group]
-                index = slot.astype(jnp.int32) - (1 + which * face_chunks * LANES)
+                index = found[group].astype(jnp.int32) - (1 + which * face_chunks * LANES)
                 got = lookup(
-                    [row_of(face_recv.at[step, which], c) for c in range(6)], index, face_chunks
+                    [row_of(face_scaled.at[which], c) for c in range(6)], index, face_chunks
                 )
                 for c in range(6):
-                    parts[c][group] = parts[c][group] + factor * got[c]
+                    parts[c][group] = parts[c][group] + got[c]
         else:
 
             def arrived(at, q):
@@ -487,6 +487,7 @@
             pltpu.VMEM((8 * elems, LANES), f32),
             pltpu.VMEM((STEPS, 2, 8, face_chunks * LANES), f32),
             pltpu.VMEM((STEPS, 2, 8, face_chunks * LANES), f32),
+            pltpu.VMEM((2, 8, face_chunks * LANES), f32),
             pltpu.VMEM((n_event, 2, cols, LANES), f32),
             pltpu.VMEM((peers, 2, cols, LANES), f32),
             pltpu.SemaphoreType.DMA((STEPS, 2)),

time: 18.2 us -> 18.4 us (1.011)
  Pallas kernels: 17.3 us -> 17.6 us
    pallas_call x1, Pallas kernels: 16.6 us -> 16.9 us  [shards(): forward, adjoint, kernels = hand_out(call(*operands))]
where the time goes in v4:
time: 18.4 us; the launch traced here: 18.2 us
  Pallas kernels  17.6 us (96%)
  between operations  0.64 us (3%)
    pallas_call x1, Pallas kernels, shards(): forward, adjoint, kernels = hand_out(call(*operands))  16.9 us
    pallas_call x1, Pallas kernels, hand_out(): pl.pallas_call(copy_out, out_shape=tuple((jax.ShapeDtypeStruct(v.shape, v...  0.65 us

profile of v4, /device:TPU:0, one launch (start us, length us, event | category | flops | bytes accessed | tf_op | source)
XLA Modules:
  0.0 18.2 jit_solution(9629733722847488885)
XLA Ops:
  0.6 16.9 %shard_map.157 = (f32[3,1,2601]{2,1,0:T(1,128)S(1)}, f32[3,1,2601]{2,1,0:T(1,128)S(1)}, f32[2,8,125]{2,1,0:T(8,128)S(1)}) custom-call(f32[3,1,2601]{2,1,0:T(1,128)} %bitcast.12, f32[3,1,2601]{2,1,0:T(1,128)} %bitcast.13, f32[3,1,2601]{2,1,0:T(1,128)} %bitcast.14, f32[3,1,2601]{2,1,0:T(1,128)} %bitcast.15, s32[32,125]{1,0:T(8,128)} %bitcast.16, ...), custom_call_target="tpu_custom_call" | custom-call | tf_op jit(solution)/shard_map/pallas_call | solution.py:502
  17.6 0.7 %shard_map.158 = (f32[3,1,2601]{2,1,0:T(1,128)}, f32[3,1,2601]{2,1,0:T(1,128)}, f32[2,8,125]{2,1,0:T(8,128)}) custom-call(f32[3,1,2601]{2,1,0:T(1,128)S(1)} %get-tuple-element.9.refs_0_, f32[3,1,2601]{2,1,0:T(1,128)S(1)} %get-tuple-element.10.refs_1_, f32[2,8,125]{2,1,0:T(8,128)S(1)} %get-tuple-element.11.refs_2_), custom_call_target="tpu_custom_call" | custom-call | tf_op jit(solution)/shard_map/pallas_call | solution.py:409

commit v5 on v4

--- a/solution.py
+++ b/solution.py
@@ -128,6 +128,9 @@
     my_event = lax.axis_index("event")
     following = lax.rem(me + 1, n_mesh)
     previous = lax.rem(me + n_mesh - 1, n_mesh)
+    has_previous = me > 0
+    has_following = me < n_mesh - 1
+    face_recv[...] = jnp.zeros_like(face_recv)
     barrier = pltpu.get_barrier_semaphore()
     for other in (following, previous):
         pl.semaphore_signal(
@@ -212,6 +215,17 @@
         for k in range(slabs):
             out[:, k * WIDE : (k + 1) * WIDE] = total[8 * k : 8 * k + 8]
 
+    def finish(copies):
+        @pl.when(has_previous)
+        def _():
+            copies[0].wait_send()
+            copies[1].wait_recv()
+
+        @pl.when(has_following)
+        def _():
+            copies[1].wait_send()
+            copies[0].wait_recv()
+
     def element_index(group):
         return rows[group * 8 : group * 8 + 8, :]
 
@@ -223,7 +237,7 @@
                 parts[c].append(got[c])
         return parts
 
-    for i in (0, 2, 12, 7, 8, 13, 11, 1, 3, 9):
+    for i in (0, 2):
         loads[i].wait()
     for c in range(3):
         waves[c : c + 1, 0:points] = fwd_now[c]
@@ -231,6 +245,8 @@
     parts = at_elements(waves)
     for e in range(elems + 1):
         spread(e)
+    for i in (12, 7, 8):
+        loads[i].wait()
     kappa_buf[:, 0:125] = bulk_mod[...]
     mu_buf[:, 0:125] = shear_mod[...]
     kappa = kappa_buf[...]
@@ -267,9 +283,13 @@
                     c = f * 3 + second
                     stress_buf[c * elems : (c + 1) * elems, lanes_of(first)] = tension
 
+        if step == 0:
+            loads[13].wait()
         force_buf[0 : 6 * elems, :] = product(stress_buf[...], back[...])
         for e in range(elems):
             place(e, force_buf[pl.ds(e, 8, stride=elems), :])
+        if step == 0:
+            loads[11].wait()
         injected = jnp.concatenate(
             [jnp.zeros((3, LANES), f32), source[0, :, step, :], jnp.zeros((2, LANES), f32)], 0
         )
@@ -294,8 +314,9 @@
                 device_id={"mesh": other, "event": my_event},
                 device_id_type=MESH,
             )
-            copy.start()
             copies.append(copy)
+        pl.when(has_previous)(copies[0].start)
+        pl.when(has_following)(copies[1].start)
 
         bulk = bulk - KERNEL_WEIGHT * kappa * divs[0] * divs[1]
         both = {key: devs[0][key] * devs[1][key] for key in devs[0]}
@@ -321,6 +342,8 @@
                 pending.append(copy)
 
         if step == 0:
+            for i in (1, 3, 9):
+                loads[i].wait()
             for c in range(3):
                 before[c : c + 1, 0:points] = fwd_prev[c]
                 before[3 + c : 4 + c, 0:points] = adj_prev[c]
@@ -328,7 +351,7 @@
             later[...] = 2.0 * waves[...] - before[...] + scale_all[...] * forces[...]
             parts = at_elements(later)
             number = lax.broadcasted_iota(jnp.int32, tile, 1)
-            for which, inside in ((0, me > 0), (1, me < n_mesh - 1)):
+            for which, inside in ((0, has_previous), (1, has_following)):
                 for k in range(face_chunks):
                     at = elems + 1 + which * face_chunks + k
                     spread(at)
@@ -340,8 +363,7 @@
                 for group in range(elems // 8)
             ]
             factors = lookup([row_of(scale_all, 0)], rows[elems : elems + 8, :], chunks)[0]
-            for copy in copies:
-                copy.wait()
+            finish(copies)
             for which in range(2):
                 for k in range(face_chunks):
                     at = 1 + which * face_chunks + k
@@ -377,8 +399,7 @@
                 before[:, span] = (
                     2.0 * now - waves[:, span] + scale_all[:, span] * forces[:, span]
                 )
-            for copy in copies:
-                copy.wait()
+            finish(copies)
             for q in range(chunks):
                 span = lanes_of(q)
                 later[:, span] = before[:, span] + scale_all[:, span] * arrived(1, q)

time: 18.4 us -> 16.4 us (0.89)
  the two profiles are of different devices: /device:TPU:0 before, /device:TPU:1 now
where the time goes in v5:
time: 16.4 us; the launch traced here: 16.1 us
  Pallas kernels  15.5 us (95%)
  between operations  0.64 us (4%)
    pallas_call x1, Pallas kernels, shards(): forward, adjoint, kernels = hand_out(call(*operands))  14.8 us
    pallas_call x1, Pallas kernels, hand_out(): pl.pallas_call(copy_out, out_shape=tuple((jax.ShapeDtypeStruct(v.shape, v...  0.65 us

profile of v5, /device:TPU:1, one launch (start us, length us, event | category | flops | bytes accessed | tf_op | source)
XLA Modules:
  0.0 16.1 jit_solution(6156994438894762439)
XLA Ops:
  0.6 14.8 %shard_map.157 = (f32[3,1,2601]{2,1,0:T(1,128)S(1)}, f32[3,1,2601]{2,1,0:T(1,128)S(1)}, f32[2,8,125]{2,1,0:T(8,128)S(1)}) custom-call(f32[3,1,2601]{2,1,0:T(1,128)} %bitcast.12, f32[3,1,2601]{2,1,0:T(1,128)} %bitcast.13, f32[3,1,2601]{2,1,0:T(1,128)} %bitcast.14, f32[3,1,2601]{2,1,0:T(1,128)} %bitcast.15, s32[32,125]{1,0:T(8,128)} %bitcast.16, ...), custom_call_target="tpu_custom_call" | custom-call | tf_op jit(solution)/shard_map/pallas_call | solution.py:523
  15.5 0.7 %shard_map.158 = (f32[3,1,2601]{2,1,0:T(1,128)}, f32[3,1,2601]{2,1,0:T(1,128)}, f32[2,8,125]{2,1,0:T(8,128)}) custom-call(f32[3,1,2601]{2,1,0:T(1,128)S(1)} %get-tuple-element.9.refs_0_, f32[3,1,2601]{2,1,0:T(1,128)S(1)} %get-tuple-element.10.refs_1_, f32[2,8,125]{2,1,0:T(8,128)S(1)} %get-tuple-element.11.refs_2_), custom_call_target="tpu_custom_call" | custom-call | tf_op jit(solution)/shard_map/pallas_call | solution.py:430

commit v6 on v5

--- a/solution.py
+++ b/solution.py
@@ -283,6 +283,29 @@
                     c = f * 3 + second
                     stress_buf[c * elems : (c + 1) * elems, lanes_of(first)] = tension
 
+        bulk = bulk - KERNEL_WEIGHT * kappa * divs[0] * divs[1]
+        both = {key: devs[0][key] * devs[1][key] for key in devs[0]}
+        paired = both[0, 0] + both[1, 1] + both[2, 2]
+        paired = paired + 2.0 * (both[0, 1] + both[0, 2] + both[1, 2])
+        shear = shear - 2.0 * KERNEL_WEIGHT * mu * paired
+
+        if step == STEPS - 1:
+            for owner in range(n_event):
+                kern_send[owner, 0] = bulk[owner * cols : (owner + 1) * cols]
+                kern_send[owner, 1] = shear[owner * cols : (owner + 1) * cols]
+            for hop in range(1, n_event):
+                peer = lax.rem(my_event + hop, n_event)
+                copy = pltpu.make_async_remote_copy(
+                    src_ref=kern_send.at[peer],
+                    dst_ref=kern_recv.at[hop - 1],
+                    send_sem=kern_ssem.at[hop - 1],
+                    recv_sem=kern_rsem.at[hop - 1],
+                    device_id={"mesh": me, "event": peer},
+                    device_id_type=MESH,
+                )
+                copy.start()
+                pending.append(copy)
+
         if step == 0:
             loads[13].wait()
         force_buf[0 : 6 * elems, :] = product(stress_buf[...], back[...])
@@ -317,29 +340,6 @@
             copies.append(copy)
         pl.when(has_previous)(copies[0].start)
         pl.when(has_following)(copies[1].start)
-
-        bulk = bulk - KERNEL_WEIGHT * kappa * divs[0] * divs[1]
-        both = {key: devs[0][key] * devs[1][key] for key in devs[0]}
-        paired = both[0, 0] + both[1, 1] + both[2, 2]
-        paired = paired + 2.0 * (both[0, 1] + both[0, 2] + both[1, 2])
-        shear = shear - 2.0 * KERNEL_WEIGHT * mu * paired
-
-        if step == STEPS - 1:
-            for owner in range(n_event):
-                kern_send[owner, 0] = bulk[owner * cols : (owner + 1) * cols]
-                kern_send[owner, 1] = shear[owner * cols : (owner + 1) * cols]
-            for hop in range(1, n_event):
-                peer = lax.rem(my_event + hop, n_event)
-                copy = pltpu.make_async_remote_copy(
-                    src_ref=kern_send.at[peer],
-                    dst_ref=kern_recv.at[hop - 1],
-                    send_sem=kern_ssem.at[hop - 1],
-                    recv_sem=kern_rsem.at[hop - 1],
-                    device_id={"mesh": me, "event": peer},
-                    device_id_type=MESH,
-                )
-                copy.start()
-                pending.append(copy)
 
         if step == 0:
             for i in (1, 3, 9):

time: 16.4 us -> 15 us (0.915)
  Pallas kernels: 15.5 us -> 14.1 us
    pallas_call x1, Pallas kernels: 14.8 us -> 13.4 us  [shards(): forward, adjoint, kernels = hand_out(call(*operands))]
where the time goes in v6:
time: 15 us; the launch traced here: 14.7 us
  Pallas kernels  14.1 us (94%)
  between operations  0.64 us (4%)
    pallas_call x1, Pallas kernels, shards(): forward, adjoint, kernels = hand_out(call(*operands))  13.4 us
    pallas_call x1, Pallas kernels, hand_out(): pl.pallas_call(copy_out, out_shape=tuple((jax.ShapeDtypeStruct(v.shape, v...  0.65 us

profile of v6, /device:TPU:1, one launch (start us, length us, event | category | flops | bytes accessed | tf_op | source)
XLA Modules:
  0.0 14.7 jit_solution(17986550715957044244)
XLA Ops:
  0.6 13.4 %shard_map.157 = (f32[3,1,2601]{2,1,0:T(1,128)S(1)}, f32[3,1,2601]{2,1,0:T(1,128)S(1)}, f32[2,8,125]{2,1,0:T(8,128)S(1)}) custom-call(f32[3,1,2601]{2,1,0:T(1,128)} %bitcast.12, f32[3,1,2601]{2,1,0:T(1,128)} %bitcast.13, f32[3,1,2601]{2,1,0:T(1,128)} %bitcast.14, f32[3,1,2601]{2,1,0:T(1,128)} %bitcast.15, s32[32,125]{1,0:T(8,128)} %bitcast.16, ...), custom_call_target="tpu_custom_call" | custom-call | tf_op jit(solution)/shard_map/pallas_call | solution.py:523
  14.1 0.7 %shard_map.158 = (f32[3,1,2601]{2,1,0:T(1,128)}, f32[3,1,2601]{2,1,0:T(1,128)}, f32[2,8,125]{2,1,0:T(8,128)}) custom-call(f32[3,1,2601]{2,1,0:T(1,128)S(1)} %get-tuple-element.9.refs_0_, f32[3,1,2601]{2,1,0:T(1,128)S(1)} %get-tuple-element.10.refs_1_, f32[2,8,125]{2,1,0:T(8,128)S(1)} %get-tuple-element.11.refs_2_), custom_call_target="tpu_custom_call" | custom-call | tf_op jit(solution)/shard_map/pallas_call | solution.py:430
